TPU v7x, 32 devices: a whole 2x2x4 slice. The times are simulated.
32 devices in a mesh: groups: 2 (over x), wide: 16 (over z, y, core).
Axes of the slice: x: 2, y: 2, z: 4, core: 2. Of those that a mesh axis runs over, the one named last changes fastest.
Arguments:
- queries: bfloat16 [128, 32, 128], P(('groups', 'wide')), parts along dimension 0, may hold values from -6 to 6
- candidates: int32 [128, 192], P('groups', 'wide'), parts along dimension 0, may hold values from -1 to 47, as said below
- codes: int32 [1536, 128], P(('groups', 'wide')), parts along dimension 0, may hold values from 0 to 4095
- residual_words: int32 [1536, 16, 128], P(('groups', 'wide')), parts along dimension 0, may hold values from 0 to 65535
- lengths: int32 [1536], P(('groups', 'wide')), parts along dimension 0, may hold values from 32 to 128, as said below
- centroids: float32 [131072, 128], P(('groups', 'wide')), parts along dimension 0, may hold values from -0.5 to 0.5
- bucket_values: float32 [4, 128], replicated, may hold values from -0.35355338 to 0.35355338
Outputs:
- scores: float32 [128, 192], P(('groups', 'wide')), parts along dimension 0
There are 2 independent parts, one for each index of `groups`. A program takes and returns all parts, laid end to end along the dimension named above; an argument that names none is the same for every part. Nothing has to cross between parts.
Inputs may be any that keep to these rules, and one draw needn't show every extreme that they name: `candidates`: -1 marks an empty slot; in each block of 12 slots of one query at one shard the live slots come first, and every query fills all 12 slots at some shard. `lengths`: every shard holds a passage of 128 tokens.
All inputs are finite; a program needn't handle non-finite values.
Results may differ from a plain program's by a relative error of at most 0.00034.
Values may be sent and summed in bfloat16 or wider, within the bound.
A program may use at most 64 MiB of HBM per device.

v0:
```python
import math

import jax
import jax.numpy as jnp
from jax import lax
from jax.sharding import PartitionSpec as P

epsilon = 1e-06


def unit_rows(values_in):
    values = values_in.astype(jnp.float32)
    return values / jnp.sqrt(jnp.sum(values * values, axis=-1, keepdims=True) + epsilon)


def decode(codes, words, centroids, bucket_values):
    width = centroids.shape[1]
    expanded = jnp.repeat(words, 8, axis=-2)
    powers = jnp.power(4, jnp.arange(width, dtype=jnp.int32) % 8).astype(jnp.int32)
    buckets = jnp.swapaxes(expanded // powers[:, None] % 4, -1, -2)
    residual = jnp.zeros(buckets.shape, jnp.float32)
    for level in range(4):
        residual = residual + jnp.where(buckets == level, bucket_values[level], jnp.float32(0.0))
    vectors = centroids[codes] + residual
    return unit_rows(vectors).astype(jnp.bfloat16)


def on_device(queries, candidates, codes, residual_words, lengths, centroids, bucket_values):
    query_unit = unit_rows(queries).astype(jnp.bfloat16)
    decoded = decode(codes, residual_words, centroids, bucket_values)
    passage_count = decoded.shape[0]
    positions = jnp.arange(decoded.shape[1], dtype=jnp.int32)
    within = positions[None, :] < lengths[:, None]
    passage_index = jnp.arange(passage_count, dtype=jnp.int32)
    group_limit = 16

    def score_group(paired):
        query_group, slot_group = paired
        similar = jnp.einsum(
            "bid,pjd->bipj", query_group, decoded, preferred_element_type=jnp.float32
        )
        maxima = jnp.max(jnp.where(within[None, None, :, :], similar, jnp.float32(-1e30)), axis=-1)
        passage_scores = jnp.mean(maxima, axis=1)
        picker = (slot_group[:, :, None] == passage_index[None, None, :]).astype(jnp.float32)
        picked = jnp.sum(picker * passage_scores[:, None, :], axis=-1)
        return jnp.where(slot_group >= 0, picked, jnp.float32(0.0))

    query_rows = lax.all_gather(query_unit, "wide", axis=0, tiled=True)
    row_count = query_rows.shape[0]
    group_size = math.gcd(row_count, group_limit)
    grouped = (
        query_rows.reshape((row_count // group_size, group_size) + query_rows.shape[1:]),
        candidates.reshape((row_count // group_size, group_size, candidates.shape[1])),
    )
    local_scores = lax.map(score_group, grouped).reshape((row_count, candidates.shape[1]))
    return lax.all_to_all(local_scores, "wide", split_axis=0, concat_axis=1, tiled=True)


def solution(mesh):
    in_specs = (
        P(("groups", "wide"), None, None),
        P("groups", "wide"),
        P(("groups", "wide"), None),
        P(("groups", "wide"), None, None),
        P(("groups", "wide")),
        P(("groups", "wide"), None),
        P(),
    )
    out_specs = P(("groups", "wide"), None)
    return jax.shard_map(
        on_device, mesh=mesh, in_specs=in_specs, out_specs=out_specs, check_vma=False
    )
```

profile of v0, /device:TPU:0, one launch (start us, length us, event | category | flops | bytes accessed | tf_op | source)
XLA Modules:
  0.0 122.7 jit_solution(1042459967537335176)
XLA Ops:
  0.0 0.0 copy-start
  0.0 0.9 slice_bitcast_fusion.3
  0.9 0.7 fusion.16
  1.7 0.0 copy-done
  1.7 20.9 %gather_fusion = f32[6144,128]{1,0:T(8,128)} fusion(f32[4096,128]{1,0:T(8,128)S(1)} %copy-done, s32[6144]{0:T(1024)S(1)} %fusion.16), kind=kCustom, calls=%fused_computation | custom fusion | bytes 6316032 | tf_op jit(solution)/shard_map/gather | solution.py:24
  22.6 0.0 copy-start.1
  22.6 3.6 %copy.21 = f32[48,128,128]{1,2,0:T(8,128)} copy(f32[48,128,128]{2,1,0:T(8,128)} %bitcast.64) | data formatting | bytes 6291456 | tf_op jit(solution)/shard_map/gather | solution.py:24
  26.2 0.0 copy-done.1
  26.2 35.0 %multiply_reduce_fusion = (f32[48,128]{1,0:T(8,128)S(1)}, f32[48,128,128]{1,2,0:T(8,128)S(1)}) fusion(f32[48,128,128]{1,2,0:T(8,128)} %copy.21, f32[128]{0:T(128)S(1)} %get-tuple-element.93, f32[128]{0:T(128)S(1)} %get-tuple-element.94, f32[128]{0:T(128)S(1)} %get-tuple-element.92, f32[128]{0:T(128)S(1)} %get-tuple-element.91, s32[128]{0:T(128)S(1)} %get-tuple-element.95, ...), kind=kLoop, calls=%fused_computation.27 | loop fusion | flops 25946112 | bytes 6712320 | tf_op jit(solution)/shard_map/reduce_sum | solution.py:13
  61.2 0.0 copy-start.2
  61.2 0.0 copy-start.4
  61.2 0.0 copy-start.3
  61.2 1.6 %divide_convert_fusion = bf16[48,128,128]{1,2,0:T(8,128)(2,1)} fusion(f32[48,128,128]{1,2,0:T(8,128)S(1)} %get-tuple-element.90, f32[48,128]{1,0:T(8,128)S(1)} %add_sqrt_fusion), kind=kLoop, calls=%fused_computation.26 | loop fusion | flops 1572864 | bytes 4743168 | tf_op jit(solution)/shard_map/convert_element_type | solution.py:25
  62.8 2.6 %copy.22 = bf16[48,128,128]{2,1,0:T(8,128)(2,1)} copy(bf16[48,128,128]{1,2,0:T(8,128)(2,1)} %divide_convert_fusion) | data formatting | bytes 3145728
  65.4 0.0 copy-done.2
  65.4 0.1 fusion.13
  65.5 0.1 fusion.14
  65.6 24.8 %all_gather.3 = bf16[64,32,128]{2,1,0:T(8,128)(2,1)S(1)} all-gather(bf16[4,32,128]{2,1,0:T(8,128)(2,1)S(1)} %fusion.14), channel_id=1, replica_groups=mesh['groups'=2,'wide'=16] {'wide'}, dimensions={0}, use_global_device_ids=true | all-gather | bytes 557056 | tf_op jit(solution)/shard_map/all_gather | solution.py:48
  90.4 0.0 copy-done.4
  90.4 0.1 copy.20
  90.5 0.0 copy-done.3
  90.5 22.3 %while.11 = (s32[]{:T(128)}, f32[4,16,12]{2,1,0:T(8,128)S(1)}, s32[4,16,12]{2,1,0:T(8,128)S(1)}, bf16[4,16,32,128]{3,2,1,0:T(8,128)(2,1)S(1)}, bf16[48,128,128]{...) while((s32[]{:T(128)}, f32[4,16,12]{2,1,0:T(8,128)S(1)}, ...), condition=%wide.region_6.7_spmd.clone, body=%wide.region_2.6_spmd.clone.sunk | while | flops 811631808 | bytes 1956133 | solution.py:55
  90.5 0.1 iota_compare_fusion.3
  90.6 4.9 %select_reduce_fusion.4 = f32[16,32,48]{1,2,0:T(8,128)S(1)} fusion(pred[48,128]{1,0:T(8,128)(4,1)S(1)} %iota_compare_fusion.3, bf16[48,128,128]{2,1,0:T(8,128)(2,1)} %get-tuple-element.154, bf16[4,16,32,128]{3,2,1,0:T(8,128)(2,1)S(1)} %get-tuple-element.153, s32[]{:T(128)} %get-tuple-element.142), kind=kOutput, calls=%fused_computation.3.clone.1 | convolution fusion | flops 811573248 | bytes 1808388 | tf_op jit(solution)/shard_map/while/body/eval_jaxpr/bid,pjd->bipj/dot_general | solution.py:39
  95.5 0.2 reduce_sum.49
  95.7 0.1 copy.27
  95.8 0.2 select_reduce_fusion.5
  96.0 0.1 copy.28
  96.1 0.1 iota_compare_fusion.3
  96.2 4.9 %select_reduce_fusion.4 = f32[16,32,48]{1,2,0:T(8,128)S(1)} fusion(pred[48,128]{1,0:T(8,128)(4,1)S(1)} %iota_compare_fusion.3, bf16[48,128,128]{2,1,0:T(8,128)(2,1)} %get-tuple-element.154, bf16[4,16,32,128]{3,2,1,0:T(8,128)(2,1)S(1)} %get-tuple-element.153, s32[]{:T(128)} %get-tuple-element.142), kind=kOutput, calls=%fused_computation.3.clone.1 | convolution fusion | flops 811573248 | bytes 1808388 | tf_op jit(solution)/shard_map/while/body/eval_jaxpr/bid,pjd->bipj/dot_general | solution.py:39
  101.1 0.2 reduce_sum.49
  101.3 0.1 copy.27
  101.4 0.2 select_reduce_fusion.5
  101.6 0.1 copy.28
  101.7 0.1 iota_compare_fusion.3
  101.8 4.9 %select_reduce_fusion.4 = f32[16,32,48]{1,2,0:T(8,128)S(1)} fusion(pred[48,128]{1,0:T(8,128)(4,1)S(1)} %iota_compare_fusion.3, bf16[48,128,128]{2,1,0:T(8,128)(2,1)} %get-tuple-element.154, bf16[4,16,32,128]{3,2,1,0:T(8,128)(2,1)S(1)} %get-tuple-element.153, s32[]{:T(128)} %get-tuple-element.142), kind=kOutput, calls=%fused_computation.3.clone.1 | convolution fusion | flops 811573248 | bytes 1808388 | tf_op jit(solution)/shard_map/while/body/eval_jaxpr/bid,pjd->bipj/dot_general | solution.py:39
  106.7 0.2 reduce_sum.49
  106.9 0.1 copy.27
  107.0 0.2 select_reduce_fusion.5
  107.2 0.1 copy.28
  107.3 0.1 iota_compare_fusion.3
  107.3 4.9 %select_reduce_fusion.4 = f32[16,32,48]{1,2,0:T(8,128)S(1)} fusion(pred[48,128]{1,0:T(8,128)(4,1)S(1)} %iota_compare_fusion.3, bf16[48,128,128]{2,1,0:T(8,128)(2,1)} %get-tuple-element.154, bf16[4,16,32,128]{3,2,1,0:T(8,128)(2,1)S(1)} %get-tuple-element.153, s32[]{:T(128)} %get-tuple-element.142), kind=kOutput, calls=%fused_computation.3.clone.1 | convolution fusion | flops 811573248 | bytes 1808388 | tf_op jit(solution)/shard_map/while/body/eval_jaxpr/bid,pjd->bipj/dot_general | solution.py:39
  112.3 0.2 reduce_sum.49
  112.5 0.1 copy.27
  112.6 0.2 select_reduce_fusion.5
  112.8 0.1 copy.28
  112.8 9.2 %all_to_all.19 = f32[16,4,12]{2,1,0:T(4,128)S(1)} all-to-all(f32[16,4,12]{2,1,0:T(4,128)S(1)} %bitcast.68), channel_id=1, replica_groups=mesh['groups'=2,'wide'=16] {'wide'}, dimensions={0} | all-to-all | bytes 6144 | tf_op jit(solution)/shard_map/all_to_all | solution.py:56
  122.0 0.7 all_to_all.17
  (17 shorter events, 0.1 us)
Async XLA Ops:
  0.0 1.7 %copy-start = (f32[4096,128]{1,0:T(8,128)S(1)}, f32[4096,128]{1,0:T(8,128)}, u32[]{:S(2)}) copy-start(f32[4096,128]{1,0:T(8,128)} %param.14) | copy-start | bytes 6291460
  22.6 3.6 %copy-start.1 = (s32[48,16,128]{2,1,0:T(8,128)S(1)}, s32[48,16,128]{2,1,0:T(8,128)}, u32[]{:S(2)}) copy-start(s32[48,16,128]{2,1,0:T(8,128)} %param.12) | copy-start | bytes 1179652
  61.2 4.2 %copy-start.2 = (bf16[4,32,128]{2,1,0:T(8,128)(2,1)S(1)}, bf16[4,32,128]{2,1,0:T(8,128)(2,1)}, u32[]{:S(2)}) copy-start(bf16[4,32,128]{2,1,0:T(8,128)(2,1)} %param.9) | copy-start | bytes 98308
  61.2 29.2 %copy-start.4 = (s32[64,12]{0,1:T(8,128)S(1)}, s32[64,12]{0,1:T(8,128)}, u32[]{:S(2)}) copy-start(s32[64,12]{0,1:T(8,128)} %param.10) | copy-start | bytes 9220
  61.2 29.3 %copy-start.3 = (s32[48]{0:T(128)S(1)}, s32[48]{0:T(128)}, u32[]{:S(2)}) copy-start(s32[48]{0:T(128)} %param.13) | copy-start | bytes 580
where the time goes:
time: 123 us
  other arithmetic  39.3 us (32%)
  blocking collectives  34 us (28%)
  local copies, waits for them, and re-layouts  29.5 us (24%)
  matrix products  19.8 us (16%)
    reduce_sum x2, other arithmetic, unit_rows(): jnp.sum(values * values, axis=-1, keepdims=True) + epsilon  35.1 us
    all_gather x1, blocking collectives, on_device(): query_rows = lax.all_gather(query_unit, 'wide', axis=0, tiled=True)  24.8 us
    gather x2, local copies, waits for them, and re-layouts, decode(): vectors = centroids[codes] + residual  24.5 us
    dot_general x4, matrix products, score_group(): jnp.einsum('bid,pjd->bipj', query_group, decoded, preferred_element_type=...  19.8 us
    all_to_all x1, blocking collectives, on_device(): lax.all_to_all(local_scores, 'wide', split_axis=0, concat_axis=1, tiled=T...  9.2 us
    unnamed x12, local copies, waits for them, and re-layouts  2.72 us

commit v1 on v0

v1 whole, which is shorter than its diff:
```python
import functools

import jax
import jax.numpy as jnp
from jax import lax
from jax.experimental import pallas as pl
from jax.experimental.pallas import tpu as pltpu
from jax.sharding import PartitionSpec as P

epsilon = 1e-06
MESH = pl.DeviceIdType.MESH


def kernel(n, q_ref, cand_ref, codes_ref, words_ref, len_ref, cent_ref, bv_ref, out_ref,
           allq, flat, pick4, raw_a, raw_b, dec, best, snd, rcv,
           send1, recv1, send2, recv2, send3, recv3):
    chips = n // 2
    me = lax.axis_index("wide")
    chip, core = me // 2, lax.rem(me, 2)
    sibling = chip * 2 + 1 - core
    passages, plen = codes_ref.shape
    rows = q_ref.shape[0]
    width = q_ref.shape[1]
    cand = cand_ref.shape[1]
    per = snd.shape[1]

    barrier = pltpu.get_barrier_semaphore()

    def greet(step, carry):
        pl.semaphore_signal(barrier, inc=1, device_id={"wide": lax.rem(me + step, n)}, device_id_type=MESH)
        return carry

    lax.fori_loop(1, n, greet, 0)

    q = q_ref[...].astype(jnp.float32)
    q = q * lax.rsqrt(jnp.sum(q * q, axis=-1, keepdims=True) + epsilon)
    allq[chip, core] = q.astype(jnp.bfloat16)

    pl.semaphore_wait(barrier, n - 1)

    def to_chip(step):
        other = lax.rem(chip + step, chips)
        return pltpu.make_async_remote_copy(
            src_ref=allq.at[chip, core], dst_ref=allq.at[chip, core],
            send_sem=send1.at[other], recv_sem=recv1.at[chip],
            device_id={"wide": other * 2 + core}, device_id_type=MESH)

    def from_chip(step):
        other = lax.rem(chip + step, chips)
        return pltpu.make_async_remote_copy(
            src_ref=allq.at[other, core], dst_ref=allq.at[other, core],
            send_sem=send1.at[other], recv_sem=recv1.at[other],
            device_id={"wide": other * 2 + core}, device_id_type=MESH)

    def to_sibling(step):
        other = lax.rem(chip + step, chips)
        return pltpu.make_async_remote_copy(
            src_ref=allq.at[other, core], dst_ref=allq.at[other, core],
            send_sem=send2.at[other], recv_sem=recv2.at[other],
            device_id={"wide": sibling}, device_id_type=MESH)

    def from_sibling(step):
        other = lax.rem(chip + step, chips)
        return pltpu.make_async_remote_copy(
            src_ref=allq.at[other, 1 - core], dst_ref=allq.at[other, 1 - core],
            send_sem=send2.at[other], recv_sem=recv2.at[other],
            device_id={"wide": sibling}, device_id_type=MESH)

    for step in range(1, chips):
        to_chip(step).start()
    to_sibling(0).start()

    row = lax.broadcasted_iota(jnp.int32, (128, width), 0)
    col = lax.broadcasted_iota(jnp.int32, (128, width), 1)
    holds = (row % 16 == col // 8) & ((row // 16) % 2 == (col // 4) % 2)
    for inner in range(4):
        pick4[inner] = jnp.where(holds & (row // 32 == inner), 1.0, 0.0).astype(jnp.bfloat16)

    def turn(group, carry):
        parts = []
        for inner in range(4):
            word = words_ref[group * 4 + inner]
            parts += [word & 255, word >> 8]
        both = jnp.concatenate(parts, axis=0).astype(jnp.float32)
        flat[group] = jnp.transpose(both).astype(jnp.bfloat16)
        return carry

    lax.fori_loop(0, passages // 4, turn, 0)

    shift = 2 * (lax.broadcasted_iota(jnp.int32, (plen, width), 1) % 4)
    low_bit = jnp.left_shift(jnp.int32(1), shift)
    high_bit = jnp.left_shift(jnp.int32(2), shift)
    place = lax.broadcasted_iota(jnp.int32, (plen, width), 0)

    def fetch(p, raw):
        for start in range(0, plen, 8):
            got = [cent_ref[codes_ref[p, start + j]] for j in range(8)]
            for j in range(8):
                raw[start + j:start + j + 1, :] = got[j]

    def decode(p, raw):
        byte = jnp.dot(flat[p // 4], pick4[lax.rem(p, 4)], preferred_element_type=jnp.float32).astype(jnp.int32)
        low = (byte & low_bit) != 0
        high = (byte & high_bit) != 0
        residual = jnp.where(high, jnp.where(low, bv_ref[3:4, :], bv_ref[2:3, :]),
                             jnp.where(low, bv_ref[1:2, :], bv_ref[0:1, :]))
        value = raw[...] + residual
        value = jnp.where(place < len_ref[p], value, value[0:1, :])
        value = value * lax.rsqrt(jnp.sum(value * value, axis=-1, keepdims=True) + epsilon)
        dec[pl.ds(pl.multiple_of(p * plen, plen), plen), :] = value.astype(jnp.bfloat16)

    def pair(i, carry):
        fetch(2 * i + 1, raw_b)
        decode(2 * i, raw_a)
        fetch(jnp.minimum(2 * i + 2, passages - 1), raw_a)
        decode(2 * i + 1, raw_b)
        return carry

    fetch(0, raw_a)
    half = passages // 4
    lax.fori_loop(0, half, pair, 0)
    for step in range(1, chips):
        from_chip(step).wait_recv()
        to_sibling(step).start()
    lax.fori_loop(half, passages // 2, pair, 0)
    for step in range(chips):
        from_sibling(step).wait_recv()

    group = 8
    groups = passages // group

    def score(k, carry):
        tile = allq[k].reshape(2 * rows, width)
        for g in range(groups):
            similar = lax.dot_general(dec[g * group * plen:(g + 1) * group * plen, :], tile,
                                      (((1,), (1,)), ((), ())), preferred_element_type=jnp.float32)
            best[k, g * group:(g + 1) * group, :] = jnp.max(similar.reshape(group, plen, 2 * rows), axis=1)
        return carry

    lax.fori_loop(0, chips, score, 0)

    held = 2 * per
    tokens = rows // per
    qrow = lax.broadcasted_iota(jnp.int32, (held, 2 * rows), 0)
    qcol = lax.broadcasted_iota(jnp.int32, (held, 2 * rows), 1)
    mean = jnp.where(qcol // tokens == qrow, 1.0 / tokens, 0.0).astype(jnp.bfloat16)
    lanes = snd.shape[2]
    lane = lax.broadcasted_iota(jnp.int32, (held, lanes), 1)
    slot = lane - me * cand
    ids = lax.broadcasted_iota(jnp.int32, (held, passages), 1)

    def finish(k, carry):
        full = best[k]
        top = full.astype(jnp.bfloat16)
        rest = full - top.astype(jnp.float32)
        mid = rest.astype(jnp.bfloat16)
        low = (rest - mid.astype(jnp.float32)).astype(jnp.bfloat16)
        dims = (((1,), (1,)), ((), ()))
        scores = sum(lax.dot_general(mean, part, dims, preferred_element_type=jnp.float32)
                     for part in (low, mid, top))
        chosen = cand_ref[pl.ds(pl.multiple_of(k * held, held), held), :]
        block = jnp.zeros((held, lanes), jnp.float32)
        for s in range(cand):
            one = jnp.sum(jnp.where(chosen[:, s:s + 1] == ids, scores, 0.0), axis=1, keepdims=True)
            block = jnp.where(slot == s, one, block)
        snd[2 * k] = block[:per]
        snd[2 * k + 1] = block[per:]
        return carry

    lax.fori_loop(0, chips, finish, 0, unroll=True if chips <= 8 else 4)

    def to_owner(step):
        other = lax.rem(me + step, n)
        return pltpu.make_async_remote_copy(
            src_ref=snd.at[other], dst_ref=rcv.at[me],
            send_sem=send3.at[other], recv_sem=recv3.at[me],
            device_id={"wide": other}, device_id_type=MESH)

    def from_owner(step):
        other = lax.rem(me + step, n)
        return pltpu.make_async_remote_copy(
            src_ref=snd.at[other], dst_ref=rcv.at[other],
            send_sem=send3.at[other], recv_sem=recv3.at[other],
            device_id={"wide": other}, device_id_type=MESH)

    for step in range(1, n):
        to_owner(step).start()
    rcv[me] = snd[me]
    for step in range(1, n):
        from_owner(step).wait_recv()
    total = rcv[0]
    for o in range(1, n):
        total = total + rcv[o]
    out_ref[...] = total[:, :out_ref.shape[1]]

    for step in range(1, chips):
        to_chip(step).wait_send()
    for step in range(chips):
        to_sibling(step).wait_send()
    for step in range(1, n):
        to_owner(step).wait_send()


def on_device(n, queries, candidates, codes, residual_words, lengths, centroids, bucket_values):
    per, tokens, width = queries.shape
    passages, plen = codes.shape
    chips = n // 2
    slots = n * candidates.shape[1]
    lanes = -(-slots // 128) * 128
    rows = per * tokens
    vmem = pl.BlockSpec(memory_space=pltpu.VMEM)
    smem = pl.BlockSpec(memory_space=pltpu.SMEM)
    dma = pltpu.SemaphoreType.DMA
    return pl.pallas_call(
        functools.partial(kernel, n),
        out_shape=jax.ShapeDtypeStruct((per, slots), jnp.float32),
        in_specs=[vmem, vmem, smem, vmem, smem, vmem, vmem],
        out_specs=vmem,
        scratch_shapes=[
            pltpu.VMEM((chips, 2, rows, width), jnp.bfloat16),
            pltpu.VMEM((passages // 4, plen, 128), jnp.bfloat16),
            pltpu.VMEM((4, 128, width), jnp.bfloat16),
            pltpu.VMEM((plen, width), jnp.float32),
            pltpu.VMEM((plen, width), jnp.float32),
            pltpu.VMEM((passages * plen, width), jnp.bfloat16),
            pltpu.VMEM((chips, passages, 2 * rows), jnp.float32),
            pltpu.VMEM((n, per, lanes), jnp.float32),
            pltpu.VMEM((n, per, lanes), jnp.float32),
            dma((chips,)), dma((chips,)), dma((chips,)), dma((chips,)), dma((n,)), dma((n,)),
        ],
        compiler_params=pltpu.CompilerParams(
            collective_id=0, has_side_effects=True, vmem_limit_bytes=48 * 1024 * 1024),
    )(queries.reshape(rows, width), candidates, codes, residual_words, lengths,
      centroids.reshape(centroids.shape[0], 1, width), bucket_values)


def solution(mesh):
    in_specs = (
        P(("groups", "wide"), None, None),
        P("groups", "wide"),
        P(("groups", "wide"), None),
        P(("groups", "wide"), None, None),
        P(("groups", "wide")),
        P(("groups", "wide"), None),
        P(),
    )
    return jax.shard_map(
        functools.partial(on_device, mesh.shape["wide"]), mesh=mesh, in_specs=in_specs,
        out_specs=P(("groups", "wide"), None), check_vma=False
    )
```

time: 123 us -> 40.4 us (0.33)
  other arithmetic: 39.3 us -> 0 us
  blocking collectives: 34 us -> 0 us
  Pallas kernels: 0 us -> 33.2 us
  local copies, waits for them, and re-layouts: 29.5 us -> 6.79 us
  matrix products: 19.8 us -> 0 us
    reduce_sum x10 -> x0, other arithmetic: 36.5 us -> none  [the longest x2 35.1 us: unit_rows(): jnp.sum(values * values, axis=-1, keepdims=True) + epsilon]
    pallas_call x0 -> x1, Pallas kernels: none -> 33.2 us  [on_device(): pl.pallas_call(functools.partial(kernel, n), out_shape=jax.ShapeDtypeStru...]
    all_gather x1 -> x0, blocking collectives: 24.8 us -> none  [on_device(): query_rows = lax.all_gather(query_unit, 'wide', axis=0, tiled=True)]
    gather x2 -> x0, local copies, waits for them, and re-layouts: 24.5 us -> none  [decode(): vectors = centroids[codes] + residual]
    dot_general x4 -> x0, matrix products: 19.8 us -> none  [score_group(): jnp.einsum('bid,pjd->bipj', query_group, decoded, preferred_element_type=...]
    all_to_all x1 -> x0, blocking collectives: 9.2 us -> none  [on_device(): lax.all_to_all(local_scores, 'wide', split_axis=0, concat_axis=1, tiled=T...]
    unnamed x12 -> x14, local copies, waits for them, and re-layouts: 2.72 us -> 6.79 us
    convert_element_type x2 -> x0, other arithmetic: 1.67 us -> none  [the longest x1 1.57 us: decode(): return unit_rows(vectors).astype(jnp.bfloat16)]
where the time goes in v1:
time: 40.4 us; the launch traced here: 40 us
  Pallas kernels  33.2 us (82%)
  local copies, waits for them, and re-layouts  6.79 us (17%)
    pallas_call x1, Pallas kernels, on_device(): pl.pallas_call(functools.partial(kernel, n), out_shape=jax.ShapeDtypeStru...  33.2 us
    unnamed x14, local copies, waits for them, and re-layouts  6.79 us

profile of v1, /device:TPU:0, one launch (start us, length us, event | category | flops | bytes accessed | tf_op | source)
XLA Modules:
  0.0 40.0 jit_solution(6095504309245890854)
XLA Ops:
  0.0 0.8 %copy.8.cand_ref = s32[64,12]{1,0:T(8,128)S(1)} copy(s32[64,12]{0,1:T(8,128)} %param.8) | data formatting | bytes 6144 | tf_op args[1]
  0.8 0.0 copy-start
  0.8 1.6 %copy-done = f32[4096,128]{1,0:T(8,128)S(1)} copy-done((f32[4096,128]{1,0:T(8,128)S(1)}, f32[4096,128]{1,0:T(8,128)}, u32[]{:S(2)}) %copy-start) | copy-done | bytes 2097176
  2.4 0.0 copy-start.1
  2.4 1.0 %copy-done.1 = s32[48,16,128]{2,1,0:T(8,128)S(1)} copy-done((s32[48,16,128]{2,1,0:T(8,128)S(1)}, s32[48,16,128]{2,1,0:T(8,128)}, u32[]{:S(2)}) %copy-start.1) | copy-done | bytes 393240
  3.4 0.0 copy-start.2
  3.4 0.8 %copy-done.2 = bf16[4,32,128]{2,1,0:T(8,128)(2,1)S(1)} copy-done((bf16[4,32,128]{2,1,0:T(8,128)(2,1)S(1)}, bf16[4,32,128]{2,1,0:T(8,128)(2,1)}, u32[]{:S(2)}) %copy-start.2) | copy-done | bytes 32792
  4.1 0.0 copy-start.3
  4.1 0.7 %copy-done.3 = s32[48,128]{1,0:T(8,128)S(1)} copy-done((s32[48,128]{1,0:T(8,128)S(1)}, s32[48,128]{1,0:T(8,128)}, u32[]{:S(2)}) %copy-start.3) | copy-done | bytes 24600
  4.9 0.0 copy-start.4
  4.9 0.7 %copy-done.4 = f32[4,128]{1,0:T(4,128)S(1)} copy-done((f32[4,128]{1,0:T(4,128)S(1)}, f32[4,128]{1,0:T(4,128)}, u32[]{:S(2)}) %copy-start.4) | copy-done | bytes 2072
  5.6 0.0 copy-start.5
  5.6 0.7 %copy-done.5 = s32[48]{0:T(128)S(1)} copy-done((s32[48]{0:T(128)S(1)}, s32[48]{0:T(128)}, u32[]{:S(2)}) %copy-start.5) | copy-done | bytes 216
  6.2 33.2 %shard_map.73 = f32[4,192]{1,0:T(4,128)S(1)} custom-call(bf16[128,128]{1,0:T(8,128)(2,1)S(1)} %bitcast.3, s32[64,12]{1,0:T(8,128)S(1)} %copy.8.cand_ref, s32[48,128]{1,0:T(8,128)S(1)} %copy-done.3, s32[48,16,128]{2,1,0:T(8,128)S(1)} %copy-done.1, s32[48]{0:T(128)S(1)} %copy-done.5, f32[4096,1,128]{2,1,0:T(1,128)S(1)} %bitcast.2, f32[4,128]{1,0:T(4,128)S(1)} %copy-done.4), custom_call_target="tpu_custom_call" | custom-call | tf_op jit(solution)/shard_map/pallas_call | solution.py:214
  39.4 0.6 %copy.10 = f32[4,192]{1,0:T(4,128)} copy(f32[4,192]{1,0:T(4,128)S(1)} %shard_map.73) | data formatting | bytes 6144
Async XLA Ops:
  0.8 1.6 %copy-start = (f32[4096,128]{1,0:T(8,128)S(1)}, f32[4096,128]{1,0:T(8,128)}, u32[]{:S(2)}) copy-start(f32[4096,128]{1,0:T(8,128)} %param.12) | copy-start | bytes 6291460
  2.4 1.0 %copy-start.1 = (s32[48,16,128]{2,1,0:T(8,128)S(1)}, s32[48,16,128]{2,1,0:T(8,128)}, u32[]{:S(2)}) copy-start(s32[48,16,128]{2,1,0:T(8,128)} %words_ref.1) | copy-start | bytes 1179652
  3.4 0.8 %copy-start.2 = (bf16[4,32,128]{2,1,0:T(8,128)(2,1)S(1)}, bf16[4,32,128]{2,1,0:T(8,128)(2,1)}, u32[]{:S(2)}) copy-start(bf16[4,32,128]{2,1,0:T(8,128)(2,1)} %param.7) | copy-start | bytes 98308
  4.1 0.7 %copy-start.3 = (s32[48,128]{1,0:T(8,128)S(1)}, s32[48,128]{1,0:T(8,128)}, u32[]{:S(2)}) copy-start(s32[48,128]{1,0:T(8,128)} %codes_ref.1) | copy-start | bytes 73732
  4.9 0.7 %copy-start.4 = (f32[4,128]{1,0:T(4,128)S(1)}, f32[4,128]{1,0:T(4,128)}, u32[]{:S(2)}) copy-start(f32[4,128]{1,0:T(4,128)} %bv_ref.1) | copy-start | bytes 6148
  5.6 0.7 %copy-start.5 = (s32[48]{0:T(128)S(1)}, s32[48]{0:T(128)}, u32[]{:S(2)}) copy-start(s32[48]{0:T(128)} %len_ref.1) | copy-start | bytes 580

commit v2 on v1

--- a/solution.py
+++ b/solution.py
@@ -11,8 +11,8 @@
 MESH = pl.DeviceIdType.MESH
 
 
-def kernel(n, q_ref, cand_ref, codes_ref, words_ref, len_ref, cent_ref, bv_ref, out_ref,
-           allq, flat, pick4, raw_a, raw_b, dec, best, snd, rcv,
+def kernel(n, q_hbm, cand_hbm, codes_hbm, words_hbm, len_hbm, cent_hbm, bv_hbm, out_ref,
+           q_ref, cand_ref, codes_ref, words_ref, len_ref, cent_ref, bv_ref, load_sem, chosen_ref, allq, flat, pick4, raw_a, raw_b, dec, best, snd, rcv,
            send1, recv1, send2, recv2, send3, recv3):
     chips = n // 2
     me = lax.axis_index("wide")
@@ -21,8 +21,14 @@
     passages, plen = codes_ref.shape
     rows = q_ref.shape[0]
     width = q_ref.shape[1]
-    cand = cand_ref.shape[1]
+    cand = cand_ref.shape[0]
     per = snd.shape[1]
+
+    pairs = ((q_hbm, q_ref), (cent_hbm, cent_ref), (words_hbm, words_ref), (codes_hbm, codes_ref),
+             (len_hbm, len_ref), (bv_hbm, bv_ref), (cand_hbm, cand_ref))
+    loads = [pltpu.make_async_copy(a, b, load_sem.at[i]) for i, (a, b) in enumerate(pairs)]
+    for load in loads:
+        load.start()
 
     barrier = pltpu.get_barrier_semaphore()
 
@@ -32,12 +38,11 @@
 
     lax.fori_loop(1, n, greet, 0)
 
+    loads[0].wait()
     q = q_ref[...].astype(jnp.float32)
     q = q * lax.rsqrt(jnp.sum(q * q, axis=-1, keepdims=True) + epsilon)
     allq[chip, core] = q.astype(jnp.bfloat16)
 
-    pl.semaphore_wait(barrier, n - 1)
-
     def to_chip(step):
         other = lax.rem(chip + step, chips)
         return pltpu.make_async_remote_copy(
@@ -66,15 +71,15 @@
             send_sem=send2.at[other], recv_sem=recv2.at[other],
             device_id={"wide": sibling}, device_id_type=MESH)
 
-    for step in range(1, chips):
-        to_chip(step).start()
-    to_sibling(0).start()
+    for load in loads[1:]:
+        load.wait()
+    chosen_ref[...] = jnp.transpose(cand_ref[...])
 
     row = lax.broadcasted_iota(jnp.int32, (128, width), 0)
     col = lax.broadcasted_iota(jnp.int32, (128, width), 1)
     holds = (row % 16 == col // 8) & ((row // 16) % 2 == (col // 4) % 2)
     for inner in range(4):
-        pick4[inner] = jnp.where(holds & (row // 32 == inner), 1.0, 0.0).astype(jnp.bfloat16)
+        pick4[:, inner * width:(inner + 1) * width] = jnp.where(holds & (row // 32 == inner), 1.0, 0.0).astype(jnp.bfloat16)
 
     def turn(group, carry):
         parts = []
@@ -92,52 +97,57 @@
     high_bit = jnp.left_shift(jnp.int32(2), shift)
     place = lax.broadcasted_iota(jnp.int32, (plen, width), 0)
 
-    def fetch(p, raw):
-        for start in range(0, plen, 8):
-            got = [cent_ref[codes_ref[p, start + j]] for j in range(8)]
-            for j in range(8):
-                raw[start + j:start + j + 1, :] = got[j]
-
-    def decode(p, raw):
-        byte = jnp.dot(flat[p // 4], pick4[lax.rem(p, 4)], preferred_element_type=jnp.float32).astype(jnp.int32)
-        low = (byte & low_bit) != 0
-        high = (byte & high_bit) != 0
-        residual = jnp.where(high, jnp.where(low, bv_ref[3:4, :], bv_ref[2:3, :]),
-                             jnp.where(low, bv_ref[1:2, :], bv_ref[0:1, :]))
-        value = raw[...] + residual
-        value = jnp.where(place < len_ref[p], value, value[0:1, :])
-        value = value * lax.rsqrt(jnp.sum(value * value, axis=-1, keepdims=True) + epsilon)
-        dec[pl.ds(pl.multiple_of(p * plen, plen), plen), :] = value.astype(jnp.bfloat16)
+    batch = 4
+
+    def fetch(i, raw):
+        for inner in range(batch):
+            p = i * batch + inner
+            for start in range(0, plen, 8):
+                got = [cent_ref[codes_ref[p, start + j]] for j in range(8)]
+                for j in range(8):
+                    raw[inner * plen + start + j:inner * plen + start + j + 1, :] = got[j]
+
+    def decode(i, raw):
+        bytes4 = jnp.dot(flat[i], pick4[...], preferred_element_type=jnp.float32)
+        for inner in range(batch):
+            p = i * batch + inner
+            byte = bytes4[:, inner * width:(inner + 1) * width].astype(jnp.int32)
+            low = (byte & low_bit) != 0
+            high = (byte & high_bit) != 0
+            residual = jnp.where(high, jnp.where(low, bv_ref[3:4, :], bv_ref[2:3, :]),
+                                 jnp.where(low, bv_ref[1:2, :], bv_ref[0:1, :]))
+            value = raw[inner * plen:(inner + 1) * plen, :] + residual
+            value = jnp.where(place < len_ref[p], value, value[0:1, :])
+            value = value * lax.rsqrt(jnp.sum(value * value, axis=-1, keepdims=True) + epsilon)
+            dec[pl.ds(pl.multiple_of(p * plen, plen), plen), :] = value.astype(jnp.bfloat16)
+
+    last = passages // batch - 1
 
     def pair(i, carry):
         fetch(2 * i + 1, raw_b)
         decode(2 * i, raw_a)
-        fetch(jnp.minimum(2 * i + 2, passages - 1), raw_a)
+        fetch(jnp.minimum(2 * i + 2, last), raw_a)
         decode(2 * i + 1, raw_b)
         return carry
 
     fetch(0, raw_a)
-    half = passages // 4
-    lax.fori_loop(0, half, pair, 0)
+    early = 1
+    lax.fori_loop(0, early, pair, 0)
+    pl.semaphore_wait(barrier, n - 1)
     for step in range(1, chips):
-        from_chip(step).wait_recv()
-        to_sibling(step).start()
-    lax.fori_loop(half, passages // 2, pair, 0)
-    for step in range(chips):
-        from_sibling(step).wait_recv()
+        to_chip(step).start()
+    to_sibling(0).start()
+    lax.fori_loop(early, passages // (2 * batch), pair, 0)
 
     group = 8
     groups = passages // group
 
-    def score(k, carry):
+    def score(k):
         tile = allq[k].reshape(2 * rows, width)
         for g in range(groups):
             similar = lax.dot_general(dec[g * group * plen:(g + 1) * group * plen, :], tile,
                                       (((1,), (1,)), ((), ())), preferred_element_type=jnp.float32)
             best[k, g * group:(g + 1) * group, :] = jnp.max(similar.reshape(group, plen, 2 * rows), axis=1)
-        return carry
-
-    lax.fori_loop(0, chips, score, 0)
 
     held = 2 * per
     tokens = rows // per
@@ -149,7 +159,7 @@
     slot = lane - me * cand
     ids = lax.broadcasted_iota(jnp.int32, (held, passages), 1)
 
-    def finish(k, carry):
+    def finish(k):
         full = best[k]
         top = full.astype(jnp.bfloat16)
         rest = full - top.astype(jnp.float32)
@@ -158,36 +168,68 @@
         dims = (((1,), (1,)), ((), ()))
         scores = sum(lax.dot_general(mean, part, dims, preferred_element_type=jnp.float32)
                      for part in (low, mid, top))
-        chosen = cand_ref[pl.ds(pl.multiple_of(k * held, held), held), :]
+        chosen = chosen_ref[pl.ds(pl.multiple_of(k * held, held), held), :]
         block = jnp.zeros((held, lanes), jnp.float32)
         for s in range(cand):
             one = jnp.sum(jnp.where(chosen[:, s:s + 1] == ids, scores, 0.0), axis=1, keepdims=True)
             block = jnp.where(slot == s, one, block)
         snd[2 * k] = block[:per]
         snd[2 * k + 1] = block[per:]
-        return carry
-
-    lax.fori_loop(0, chips, finish, 0, unroll=True if chips <= 8 else 4)
-
-    def to_owner(step):
-        other = lax.rem(me + step, n)
+
+    def to_owner(other):
         return pltpu.make_async_remote_copy(
             src_ref=snd.at[other], dst_ref=rcv.at[me],
             send_sem=send3.at[other], recv_sem=recv3.at[me],
             device_id={"wide": other}, device_id_type=MESH)
 
-    def from_owner(step):
-        other = lax.rem(me + step, n)
+    def from_owner(other):
         return pltpu.make_async_remote_copy(
             src_ref=snd.at[other], dst_ref=rcv.at[other],
             send_sem=send3.at[other], recv_sem=recv3.at[other],
             device_id={"wide": other}, device_id_type=MESH)
 
-    for step in range(1, n):
-        to_owner(step).start()
+    def forward(step):
+        from_chip(step).wait_recv()
+        to_sibling(step).start()
+
+    def chip_at(i):
+        return lax.rem(chip + chips - i, chips)
+
+    ahead = min(2, chips - 1)
+    for i in range(1, ahead + 1):
+        forward(chips - i)
+    from_sibling(0).wait_recv()
+    score(chip)
+
+    def turn_out(i, carry):
+        @pl.when(i + ahead < chips)
+        def _():
+            forward(chips - i - ahead)
+
+        from_sibling(chips - i).wait_recv()
+        score(chip_at(i))
+        before = chip_at(i - 1)
+        finish(before)
+
+        @pl.when(i == 1)
+        def _():
+            to_owner(sibling).start()
+
+        @pl.when(i > 1)
+        def _():
+            to_owner(2 * before).start()
+            to_owner(2 * before + 1).start()
+
+        return carry
+
+    lax.fori_loop(1, chips, turn_out, 0)
+    final = chip_at(chips - 1)
+    finish(final)
+    to_owner(2 * final).start()
+    to_owner(2 * final + 1).start()
     rcv[me] = snd[me]
     for step in range(1, n):
-        from_owner(step).wait_recv()
+        from_owner(lax.rem(me + step, n)).wait_recv()
     total = rcv[0]
     for o in range(1, n):
         total = total + rcv[o]
@@ -198,7 +240,7 @@
     for step in range(chips):
         to_sibling(step).wait_send()
     for step in range(1, n):
-        to_owner(step).wait_send()
+        to_owner(lax.rem(me + step, n)).wait_send()
 
 
 def on_device(n, queries, candidates, codes, residual_words, lengths, centroids, bucket_values):
@@ -209,19 +251,27 @@
     lanes = -(-slots // 128) * 128
     rows = per * tokens
     vmem = pl.BlockSpec(memory_space=pltpu.VMEM)
-    smem = pl.BlockSpec(memory_space=pltpu.SMEM)
     dma = pltpu.SemaphoreType.DMA
     return pl.pallas_call(
         functools.partial(kernel, n),
         out_shape=jax.ShapeDtypeStruct((per, slots), jnp.float32),
-        in_specs=[vmem, vmem, smem, vmem, smem, vmem, vmem],
+        in_specs=[pl.BlockSpec(memory_space=pltpu.HBM)] * 7,
         out_specs=vmem,
         scratch_shapes=[
+            pltpu.VMEM((rows, width), queries.dtype),
+            pltpu.VMEM(candidates.shape[::-1], jnp.int32),
+            pltpu.SMEM((passages, plen), jnp.int32),
+            pltpu.VMEM(residual_words.shape, jnp.int32),
+            pltpu.SMEM((passages,), jnp.int32),
+            pltpu.VMEM((centroids.shape[0], 1, width), jnp.float32),
+            pltpu.VMEM(bucket_values.shape, jnp.float32),
+            dma((7,)),
+            pltpu.VMEM(candidates.shape, jnp.int32),
             pltpu.VMEM((chips, 2, rows, width), jnp.bfloat16),
             pltpu.VMEM((passages // 4, plen, 128), jnp.bfloat16),
-            pltpu.VMEM((4, 128, width), jnp.bfloat16),
-            pltpu.VMEM((plen, width), jnp.float32),
-            pltpu.VMEM((plen, width), jnp.float32),
+            pltpu.VMEM((128, 4 * width), jnp.bfloat16),
+            pltpu.VMEM((4 * plen, width), jnp.float32),
+            pltpu.VMEM((4 * plen, width), jnp.float32),
             pltpu.VMEM((passages * plen, width), jnp.bfloat16),
             pltpu.VMEM((chips, passages, 2 * rows), jnp.float32),
             pltpu.VMEM((n, per, lanes), jnp.float32),
@@ -230,7 +280,7 @@
         ],
         compiler_params=pltpu.CompilerParams(
             collective_id=0, has_side_effects=True, vmem_limit_bytes=48 * 1024 * 1024),
-    )(queries.reshape(rows, width), candidates, codes, residual_words, lengths,
+    )(queries.reshape(rows, width), candidates.T, codes, residual_words, lengths,
       centroids.reshape(centroids.shape[0], 1, width), bucket_values)
 
 

time: 40.4 us -> 35.1 us (0.87)
  Pallas kernels: 33.2 us -> 28 us
    pallas_call x1, Pallas kernels: 33.2 us -> 28 us  [on_device(): pl.pallas_call(functools.partial(kernel, n), out_shape=jax.ShapeDtypeStru...]
    unnamed x14 -> x15, local copies, waits for them, and re-layouts: 6.79 us -> 6.71 us
where the time goes in v2:
time: 35.1 us; the launch traced here: 34.7 us
  Pallas kernels  28 us (80%)
  local copies, waits for them, and re-layouts  6.71 us (19%)
    pallas_call x1, Pallas kernels, on_device(): pl.pallas_call(functools.partial(kernel, n), out_shape=jax.ShapeDtypeStru...  28 us
    unnamed x15, local copies, waits for them, and re-layouts  6.71 us

profile of v2, /device:TPU:0, one launch (start us, length us, event | category | flops | bytes accessed | tf_op | source)
XLA Modules:
  0.0 34.7 jit_solution(8721694051195732311)
XLA Ops:
  0.0 0.0 copy-start
  0.0 1.6 %copy-done = f32[4096,128]{1,0:T(8,128)S(1)} copy-done((f32[4096,128]{1,0:T(8,128)S(1)}, f32[4096,128]{1,0:T(8,128)}, u32[]{:S(2)}) %copy-start) | copy-done | bytes 2097176
  1.6 0.0 copy-start.1
  1.6 1.0 %copy-done.1 = s32[48,16,128]{2,1,0:T(8,128)S(1)} copy-done((s32[48,16,128]{2,1,0:T(8,128)S(1)}, s32[48,16,128]{2,1,0:T(8,128)}, u32[]{:S(2)}) %copy-start.1) | copy-done | bytes 393240
  2.6 0.0 copy-start.2
  2.6 0.8 %copy-done.2 = bf16[4,32,128]{2,1,0:T(8,128)(2,1)S(1)} copy-done((bf16[4,32,128]{2,1,0:T(8,128)(2,1)S(1)}, bf16[4,32,128]{2,1,0:T(8,128)(2,1)}, u32[]{:S(2)}) %copy-start.2) | copy-done | bytes 32792
  3.3 0.0 copy-start.3
  3.3 0.7 %copy-done.3 = s32[48,128]{1,0:T(8,128)S(1)} copy-done((s32[48,128]{1,0:T(8,128)S(1)}, s32[48,128]{1,0:T(8,128)}, u32[]{:S(2)}) %copy-start.3) | copy-done | bytes 24600
  4.1 0.0 copy-start.4
  4.1 0.7 %copy-done.4 = s32[64,12]{0,1:T(8,128)S(1)} copy-done((s32[64,12]{0,1:T(8,128)S(1)}, s32[64,12]{0,1:T(8,128)}, u32[]{:S(2)}) %copy-start.4) | copy-done | bytes 3096
  4.8 0.0 copy-start.5
  4.8 0.7 %copy-done.5 = f32[4,128]{1,0:T(4,128)S(1)} copy-done((f32[4,128]{1,0:T(4,128)S(1)}, f32[4,128]{1,0:T(4,128)}, u32[]{:S(2)}) %copy-start.5) | copy-done | bytes 2072
  5.5 0.0 copy-start.6
  5.5 0.7 %copy-done.6 = s32[48]{0:T(128)S(1)} copy-done((s32[48]{0:T(128)S(1)}, s32[48]{0:T(128)}, u32[]{:S(2)}) %copy-start.6) | copy-done | bytes 216
  6.1 28.0 %shard_map.73 = f32[4,192]{1,0:T(4,128)S(1)} custom-call(bf16[128,128]{1,0:T(8,128)(2,1)S(1)} %bitcast.4, s32[12,64]{1,0:T(8,128)S(1)} %bitcast.5, s32[48,128]{1,0:T(8,128)S(1)} %copy-done.3, s32[48,16,128]{2,1,0:T(8,128)S(1)} %copy-done.1, s32[48]{0:T(128)S(1)} %copy-done.6, f32[4096,1,128]{2,1,0:T(1,128)S(1)} %bitcast.3, f32[4,128]{1,0:T(4,128)S(1)} %copy-done.5), custom_call_target="tpu_custom_call" | custom-call | tf_op jit(solution)/shard_map/pallas_call | solution.py:255
  34.1 0.6 %copy.9 = f32[4,192]{1,0:T(4,128)} copy(f32[4,192]{1,0:T(4,128)S(1)} %shard_map.73) | data formatting | bytes 6144
Async XLA Ops:
  0.0 1.6 %copy-start = (f32[4096,128]{1,0:T(8,128)S(1)}, f32[4096,128]{1,0:T(8,128)}, u32[]{:S(2)}) copy-start(f32[4096,128]{1,0:T(8,128)} %param.12) | copy-start | bytes 6291460
  1.6 1.0 %copy-start.1 = (s32[48,16,128]{2,1,0:T(8,128)S(1)}, s32[48,16,128]{2,1,0:T(8,128)}, u32[]{:S(2)}) copy-start(s32[48,16,128]{2,1,0:T(8,128)} %words_hbm.1) | copy-start | bytes 1179652
  2.6 0.8 %copy-start.2 = (bf16[4,32,128]{2,1,0:T(8,128)(2,1)S(1)}, bf16[4,32,128]{2,1,0:T(8,128)(2,1)}, u32[]{:S(2)}) copy-start(bf16[4,32,128]{2,1,0:T(8,128)(2,1)} %param.7) | copy-start | bytes 98308
  3.3 0.7 %copy-start.3 = (s32[48,128]{1,0:T(8,128)S(1)}, s32[48,128]{1,0:T(8,128)}, u32[]{:S(2)}) copy-start(s32[48,128]{1,0:T(8,128)} %codes_hbm.1) | copy-start | bytes 73732
  4.1 0.7 %copy-start.4 = (s32[64,12]{0,1:T(8,128)S(1)}, s32[64,12]{0,1:T(8,128)}, u32[]{:S(2)}) copy-start(s32[64,12]{0,1:T(8,128)} %param.8) | copy-start | bytes 9220
  4.8 0.7 %copy-start.5 = (f32[4,128]{1,0:T(4,128)S(1)}, f32[4,128]{1,0:T(4,128)}, u32[]{:S(2)}) copy-start(f32[4,128]{1,0:T(4,128)} %bv_hbm.1) | copy-start | bytes 6148
  5.5 0.7 %copy-start.6 = (s32[48]{0:T(128)S(1)}, s32[48]{0:T(128)}, u32[]{:S(2)}) copy-start(s32[48]{0:T(128)} %len_hbm.1) | copy-start | bytes 580

commit v3 on v2

--- a/solution.py
+++ b/solution.py
@@ -196,10 +196,10 @@
         return lax.rem(chip + chips - i, chips)
 
     ahead = min(2, chips - 1)
-    for i in range(1, ahead + 1):
+    for i in range(1, min(ahead + 2, chips)):
         forward(chips - i)
-    from_sibling(0).wait_recv()
-    score(chip)
+    from_sibling(chips - 1).wait_recv()
+    score(chip_at(1))
 
     def turn_out(i, carry):
         @pl.when(i + ahead < chips)
@@ -211,22 +211,19 @@
         before = chip_at(i - 1)
         finish(before)
 
-        @pl.when(i == 1)
-        def _():
-            to_owner(sibling).start()
-
-        @pl.when(i > 1)
-        def _():
-            to_owner(2 * before).start()
-            to_owner(2 * before + 1).start()
-
-        return carry
-
-    lax.fori_loop(1, chips, turn_out, 0)
+        to_owner(2 * before).start()
+        to_owner(2 * before + 1).start()
+        return carry
+
+    lax.fori_loop(2, chips, turn_out, 0)
+    from_sibling(0).wait_recv()
+    score(chip)
     final = chip_at(chips - 1)
     finish(final)
     to_owner(2 * final).start()
     to_owner(2 * final + 1).start()
+    finish(chip)
+    to_owner(sibling).start()
     rcv[me] = snd[me]
     for step in range(1, n):
         from_owner(lax.rem(me + step, n)).wait_recv()

time: 35.1 us -> 35.3 us (level)
  no operation moved by 1% of the time
where the time goes in v3:
time: 35.3 us; the launch traced here: 34.9 us
  Pallas kernels  28.2 us (80%)
  local copies, waits for them, and re-layouts  6.71 us (19%)
    pallas_call x1, Pallas kernels, on_device(): pl.pallas_call(functools.partial(kernel, n), out_shape=jax.ShapeDtypeStru...  28.2 us
    unnamed x15, local copies, waits for them, and re-layouts  6.71 us

profile of v3, /device:TPU:0, one launch (start us, length us, event | category | flops | bytes accessed | tf_op | source)
XLA Modules:
  0.0 34.9 jit_solution(11605561358114909302)
XLA Ops:
  0.0 0.0 copy-start
  0.0 1.6 %copy-done = f32[4096,128]{1,0:T(8,128)S(1)} copy-done((f32[4096,128]{1,0:T(8,128)S(1)}, f32[4096,128]{1,0:T(8,128)}, u32[]{:S(2)}) %copy-start) | copy-done | bytes 2097176
  1.6 0.0 copy-start.1
  1.6 1.0 %copy-done.1 = s32[48,16,128]{2,1,0:T(8,128)S(1)} copy-done((s32[48,16,128]{2,1,0:T(8,128)S(1)}, s32[48,16,128]{2,1,0:T(8,128)}, u32[]{:S(2)}) %copy-start.1) | copy-done | bytes 393240
  2.6 0.0 copy-start.2
  2.6 0.8 %copy-done.2 = bf16[4,32,128]{2,1,0:T(8,128)(2,1)S(1)} copy-done((bf16[4,32,128]{2,1,0:T(8,128)(2,1)S(1)}, bf16[4,32,128]{2,1,0:T(8,128)(2,1)}, u32[]{:S(2)}) %copy-start.2) | copy-done | bytes 32792
  3.3 0.0 copy-start.3
  3.3 0.7 %copy-done.3 = s32[48,128]{1,0:T(8,128)S(1)} copy-done((s32[48,128]{1,0:T(8,128)S(1)}, s32[48,128]{1,0:T(8,128)}, u32[]{:S(2)}) %copy-start.3) | copy-done | bytes 24600
  4.1 0.0 copy-start.4
  4.1 0.7 %copy-done.4 = s32[64,12]{0,1:T(8,128)S(1)} copy-done((s32[64,12]{0,1:T(8,128)S(1)}, s32[64,12]{0,1:T(8,128)}, u32[]{:S(2)}) %copy-start.4) | copy-done | bytes 3096
  4.8 0.0 copy-start.5
  4.8 0.7 %copy-done.5 = f32[4,128]{1,0:T(4,128)S(1)} copy-done((f32[4,128]{1,0:T(4,128)S(1)}, f32[4,128]{1,0:T(4,128)}, u32[]{:S(2)}) %copy-start.5) | copy-done | bytes 2072
  5.5 0.0 copy-start.6
  5.5 0.7 %copy-done.6 = s32[48]{0:T(128)S(1)} copy-done((s32[48]{0:T(128)S(1)}, s32[48]{0:T(128)}, u32[]{:S(2)}) %copy-start.6) | copy-done | bytes 216
  6.1 28.2 %shard_map.73 = f32[4,192]{1,0:T(4,128)S(1)} custom-call(bf16[128,128]{1,0:T(8,128)(2,1)S(1)} %bitcast.4, s32[12,64]{1,0:T(8,128)S(1)} %bitcast.5, s32[48,128]{1,0:T(8,128)S(1)} %copy-done.3, s32[48,16,128]{2,1,0:T(8,128)S(1)} %copy-done.1, s32[48]{0:T(128)S(1)} %copy-done.6, f32[4096,1,128]{2,1,0:T(1,128)S(1)} %bitcast.3, f32[4,128]{1,0:T(4,128)S(1)} %copy-done.5), custom_call_target="tpu_custom_call" | custom-call | tf_op jit(solution)/shard_map/pallas_call | solution.py:252
  34.3 0.6 %copy.9 = f32[4,192]{1,0:T(4,128)} copy(f32[4,192]{1,0:T(4,128)S(1)} %shard_map.73) | data formatting | bytes 6144
Async XLA Ops:
  0.0 1.6 %copy-start = (f32[4096,128]{1,0:T(8,128)S(1)}, f32[4096,128]{1,0:T(8,128)}, u32[]{:S(2)}) copy-start(f32[4096,128]{1,0:T(8,128)} %param.12) | copy-start | bytes 6291460
  1.6 1.0 %copy-start.1 = (s32[48,16,128]{2,1,0:T(8,128)S(1)}, s32[48,16,128]{2,1,0:T(8,128)}, u32[]{:S(2)}) copy-start(s32[48,16,128]{2,1,0:T(8,128)} %words_hbm.1) | copy-start | bytes 1179652
  2.6 0.8 %copy-start.2 = (bf16[4,32,128]{2,1,0:T(8,128)(2,1)S(1)}, bf16[4,32,128]{2,1,0:T(8,128)(2,1)}, u32[]{:S(2)}) copy-start(bf16[4,32,128]{2,1,0:T(8,128)(2,1)} %param.7) | copy-start | bytes 98308
  3.3 0.7 %copy-start.3 = (s32[48,128]{1,0:T(8,128)S(1)}, s32[48,128]{1,0:T(8,128)}, u32[]{:S(2)}) copy-start(s32[48,128]{1,0:T(8,128)} %codes_hbm.1) | copy-start | bytes 73732
  4.1 0.7 %copy-start.4 = (s32[64,12]{0,1:T(8,128)S(1)}, s32[64,12]{0,1:T(8,128)}, u32[]{:S(2)}) copy-start(s32[64,12]{0,1:T(8,128)} %param.8) | copy-start | bytes 9220
  4.8 0.7 %copy-start.5 = (f32[4,128]{1,0:T(4,128)S(1)}, f32[4,128]{1,0:T(4,128)}, u32[]{:S(2)}) copy-start(f32[4,128]{1,0:T(4,128)} %bv_hbm.1) | copy-start | bytes 6148
  5.5 0.7 %copy-start.6 = (s32[48]{0:T(128)S(1)}, s32[48]{0:T(128)}, u32[]{:S(2)}) copy-start(s32[48]{0:T(128)} %len_hbm.1) | copy-start | bytes 580
